TPU v7x, 256 devices: a whole 4x4x8 slice. The times are simulated.
256 devices in a mesh: row: 8 (over y, x_lo), col: 8 (over z), depth: 4 (over x_hi, core).
Axes of the slice: x: 4 (x_hi: 2, x_lo: 2; x = x_hi * 2 + x_lo), y: 4, z: 8, core: 2. Of those that a mesh axis runs over, the one named last changes fastest.
Arguments:
- tokens: float32 [1536, 6144], P('row', 'col'), may hold values from -6 to 6
- up_weight: float32 [12288, 6144], P(('row', 'depth'), 'col'), may hold values from -0.078125 to 0.078125
- down_weight: float32 [12288, 6144], P(('row', 'depth'), 'col'), may hold values from -0.0546875 to 0.0546875
- cotangent: float32 [1536, 6144], P('row', 'col'), may hold values from -1.25 to 1.25
Outputs:
- output: float32 [1536, 6144], P('row', ('col', 'depth'))
- grad_tokens: float32 [1536, 6144], P('row', ('col', 'depth'))
- grad_up: float32 [12288, 6144], P(('row', 'depth'), 'col')
- grad_down: float32 [12288, 6144], P(('row', 'depth'), 'col')
All inputs are finite; a program needn't handle non-finite values.
Results may differ from a plain program's by a relative error of at most 0.00013.
Values sent between devices are 32-bit elements; how exact they have to be, the bound alone decides.
A program may use at most 128 MiB of HBM per device.

v0:
```python
import jax
import jax.numpy as jnp
from jax import lax
from jax.experimental import pallas as pl
from jax.experimental.pallas import tpu as pltpu
from jax.sharding import PartitionSpec as P

F32, BF16 = jnp.float32, jnp.bfloat16
root_two_pi = 0.7978845608028654
cubic_coef = 0.044715

SLOTS = 260
BLOCK, WIDTH, UNITS, CHUNK = 192, 768, 384, 24
GROUPS = (
    ((0, 0, 0), (1, 0, 0)),
    ((0, 1, 0), (1, 1, 0)),
    ((0, 0, 1), (0, 0, 3)),
    ((0, 1, 1), (0, 1, 3)),
    ((0, 0, 2), (0, 1, 2)),
    ((1, 0, 1), (1, 0, 3)),
    ((1, 1, 1), (1, 1, 3)),
    ((1, 0, 2), (1, 1, 2)),
)
FIRST_WAY = (0, 1, 0, 1, 0, 1, 0, 1)
PLACE = {block: at for at, block in enumerate(block for group in GROUPS for block in group)}
SPAN = tuple(slice(PLACE[group[0]], PLACE[group[0]] + len(group)) for group in GROUPS)
BLOCKS = tuple((g, dy) for g in range(2) for dy in range(4))
Y_FIRST = ((0, 1, 0, 1), (0, 1, 1, 0))
(
    OWN_X, OWN_Y, GY, GF, GX, SPLIT_WEIGHTS, PROD, RS_HOP, FINISH, AG_GET, F_MM, F_SIB, F_R1, F_R2, F_R3, F_R4,
    SWAP, SWAPPED, GRAD, DRAIN,
) = range(20)
ORDER = (
    (OWN_Y, 0), (OWN_X, 0), (OWN_X, 1), (SPLIT_WEIGHTS, 1), (SPLIT_WEIGHTS, 0), (PROD, 0), (GY, 0, 0, 0),
    (GX, 0, 0, 0), (GX, 0, 0, 1), (GY, 0, 1, 1), (RS_HOP, 0, 0, 2), (RS_HOP, 0, 1, 3), (GY, 0, 0, 1), (GY, 0, 1, 0),
    (GX, 1, 0, 1), (GX, 1, 0, 0), (OWN_Y, 1), (RS_HOP, 0, 0, 3), (RS_HOP, 0, 1, 4), (PROD, 2), (GF, 0, 0), (GF, 0, 1),
    (RS_HOP, 0, 0, 4), (PROD, 1), (GX, 0, 1, 0), (RS_HOP, 2, 0, 2), (RS_HOP, 2, 1, 3), (GY, 1, 0, 0), (GX, 0, 3, 0),
    (GX, 0, 1, 1), (GX, 0, 3, 1), (FINISH, 0), (GY, 1, 0, 1), (GX, 0, 2, 1), (GY, 1, 1, 0), (RS_HOP, 1, 1, 2),
    (RS_HOP, 1, 0, 3), (GX, 0, 2, 0), (GY, 1, 1, 1), (DRAIN, 16), (RS_HOP, 2, 1, 4), (RS_HOP, 2, 0, 3), (PROD, 3),
    (GF, 1, 0), (GX, 1, 3, 0), (AG_GET, 0, 1, 1), (RS_HOP, 1, 1, 3), (DRAIN, 16), (RS_HOP, 1, 0, 4), (GX, 1, 3, 1),
    (PROD, 4), (DRAIN, 16), (GX, 1, 1, 0), (DRAIN, 16), (RS_HOP, 2, 0, 4), (RS_HOP, 3, 0, 3), (RS_HOP, 3, 1, 2),
    (RS_HOP, 1, 1, 4), (RS_HOP, 4, 0, 2), (GX, 1, 2, 0), (GF, 1, 1), (RS_HOP, 4, 1, 3), (FINISH, 2), (GX, 1, 1, 1),
    (RS_HOP, 3, 0, 4), (RS_HOP, 3, 1, 3), (RS_HOP, 4, 0, 3), (FINISH, 1), (AG_GET, 2, 0, 1), (RS_HOP, 4, 1, 4),
    (AG_GET, 2, 1, 1), (RS_HOP, 3, 1, 4), (RS_HOP, 4, 0, 4), (AG_GET, 1, 0, 1), (PROD, 6), (AG_GET, 1, 1, 1),
    (GX, 1, 2, 1), (AG_GET, 2, 0, 2), (FINISH, 4), (FINISH, 3), (PROD, 5), (RS_HOP, 6, 0, 2), (AG_GET, 0, 0, 1),
    (AG_GET, 2, 0, 3), (PROD, 7), (AG_GET, 4, 0, 1), (AG_GET, 1, 1, 2), (AG_GET, 2, 1, 2), (AG_GET, 3, 1, 1),
    (AG_GET, 4, 1, 1), (AG_GET, 3, 0, 1), (F_MM, 0, 1, 0, 1), (RS_HOP, 5, 1, 2), (RS_HOP, 5, 0, 3), (AG_GET, 1, 0, 2),
    (RS_HOP, 6, 1, 3), (F_SIB, 0, 1), (GRAD, 0, 1), (AG_GET, 0, 0, 2), (RS_HOP, 6, 0, 3), (F_MM, 0, 4, 0),
    (AG_GET, 3, 1, 2), (AG_GET, 4, 1, 2), (AG_GET, 1, 1, 3), (AG_GET, 4, 0, 2), (F_R1, 0, 1), (RS_HOP, 7, 1, 2),
    (AG_GET, 3, 0, 2), (RS_HOP, 7, 0, 3), (AG_GET, 0, 1, 2), (F_MM, 0, 2, 0, 1), (RS_HOP, 5, 1, 3), (AG_GET, 1, 0, 3),
    (RS_HOP, 6, 1, 4), (F_R2, 0, 1), (F_SIB, 0, 2), (AG_GET, 0, 0, 3), (GRAD, 0, 2), (AG_GET, 4, 0, 3), (DRAIN, 16),
    (RS_HOP, 7, 1, 3), (AG_GET, 2, 1, 3), (RS_HOP, 5, 0, 4), (RS_HOP, 6, 0, 4), (F_R1, 0, 2), (RS_HOP, 5, 1, 4),
    (AG_GET, 4, 1, 3), (AG_GET, 3, 0, 3), (AG_GET, 2, 0, 4), (F_R3, 0, 1), (AG_GET, 0, 1, 3), (AG_GET, 3, 1, 3),
    (F_MM, 0, 3, 0, 1), (RS_HOP, 7, 0, 4), (GRAD, 0, 3), (RS_HOP, 7, 1, 4), (AG_GET, 4, 0, 4), (AG_GET, 0, 0, 4),
    (F_SIB, 0, 3), (AG_GET, 1, 1, 4), (F_R2, 0, 2), (FINISH, 5), (FINISH, 6), (AG_GET, 3, 1, 4), (F_MM, 0, 4, 1),
    (FINISH, 7), (F_R4, 0, 1), (F_MM, 1, 4, 0), (AG_GET, 5, 0, 1), (F_R1, 0, 3), (AG_GET, 5, 1, 1), (F_SIB, 0, 4),
    (AG_GET, 6, 0, 1), (AG_GET, 6, 1, 1), (GRAD, 0, 4), (AG_GET, 7, 1, 1), (AG_GET, 7, 0, 1), (AG_GET, 5, 0, 2),
    (AG_GET, 5, 1, 2), (F_MM, 1, 1, 0, 1), (AG_GET, 6, 1, 2), (F_R3, 0, 2), (F_R2, 0, 3), (AG_GET, 6, 0, 2),
    (F_R1, 0, 4), (AG_GET, 7, 1, 2), (AG_GET, 7, 0, 2), (F_MM, 1, 2, 0, 1), (AG_GET, 5, 1, 3), (GRAD, 1, 1),
    (AG_GET, 6, 0, 3), (AG_GET, 7, 1, 3), (AG_GET, 5, 0, 3), (F_R4, 0, 2), (F_SIB, 1, 1), (AG_GET, 6, 1, 3),
    (F_R3, 0, 3), (F_SIB, 1, 2), (AG_GET, 7, 0, 3), (F_MM, 1, 3, 0, 1), (F_R2, 0, 4), (AG_GET, 5, 1, 4),
    (AG_GET, 7, 1, 4), (AG_GET, 6, 0, 4), (F_MM, 1, 4, 1), (F_R1, 1, 1), (F_SIB, 1, 3), (F_R1, 1, 2), (F_SIB, 1, 4),
    (GRAD, 1, 2), (F_R2, 1, 1), (F_R3, 0, 4), (F_R4, 0, 3), (DRAIN, 16), (F_R1, 1, 3), (F_R1, 1, 4), (DRAIN, 16),
    (GRAD, 1, 3), (F_R3, 1, 1), (F_R2, 1, 2), (F_R4, 0, 4), (F_R2, 1, 3), (SWAP, 0), (F_R2, 1, 4), (F_R3, 1, 2),
    (DRAIN, 16), (F_R3, 1, 3), (F_R4, 1, 1), (F_R3, 1, 4), (GRAD, 1, 4), (F_R4, 1, 2), (F_R4, 1, 3), (F_R4, 1, 4),
    (SWAP, 1), (DRAIN, 16), (SWAPPED, 0), (SWAPPED, 1),
)


def gelu_parts(hidden):
    inner_arg = root_two_pi * (hidden + cubic_coef * hidden * hidden * hidden)
    bent_value = jnp.tanh(inner_arg)
    result = 0.5 * hidden * (1.0 + bent_value)
    slopes = 0.5 * (1.0 + bent_value) + 0.5 * hidden * (
        1.0 - bent_value * bent_value
    ) * root_two_pi * (1.0 + 3.0 * cubic_coef * hidden * hidden)
    return (result, slopes)


def halves(value):
    high = value.astype(BF16)
    return high, (value - high.astype(F32)).astype(BF16)


def kernel(
    tokens, up_weight, down_weight, cotangent,
    output, grad_tokens, grad_up, grad_down,
    gathered, raw, weights, partial, summed, spread, slope, fold, from_sib,
    near, far_x, far_y, last, ends, result, give, take, widths, grads,
    send_sem, recv_sem, local_sem,
):
    row, z, depth = lax.axis_index("row"), lax.axis_index("col"), lax.axis_index("depth")
    y, xl, xh, q = row // 2, row % 2, depth // 2, depth % 2
    xh_r, xh_l, xh_s = (xh + xl) % 2, (xh + xl + 1) % 2, (xh + xl + q) % 2
    sib = (row, z, xh * 2 + 1 - q)
    y_r, y_l = (((y + 1) % 4) * 2 + xl, z, depth), (((y + 3) % 4) * 2 + xl, z, depth)
    x_r, x_l = (y * 2 + 1 - xl, z, xh_r * 2 + q), (y * 2 + 1 - xl, z, xh_l * 2 + q)
    z_r, z_l = (row, (z + 1) % 8, depth), (row, (z + 7) % 8, depth)
    y_s = (((y + 1 + 2 * q) % 4) * 2 + xl, z, depth)
    x_s = (y * 2 + 1 - xl, z, xh_s * 2 + q)
    z_dev, z_sgn = (z_r, z_l), (1, 7)

    slots, pending = {}, []

    def remote(name, src, dst, device):
        at = slots.setdefault(name, len(slots))
        return pltpu.make_async_remote_copy(
            src_ref=src, dst_ref=dst, send_sem=send_sem.at[at], recv_sem=recv_sem.at[at],
            device_id=device, device_id_type=pl.DeviceIdType.MESH,
        )

    def send(name, src, dst, device):
        copy = remote(name, src, dst, device)
        copy.start()
        pending.append(copy)

    def arrive(name, dst):
        remote(name, dst, dst, sib).wait_recv()

    def rows(core, half):
        return pl.ds(pl.multiple_of(core * 96 + half * 48, 8), 48)

    def own_piece(a, g, dy, half):
        return gathered.at[a, g, (y + dy) % 4, rows(q, half)]

    def across_x(a, dy, half):
        piece = rows(q, half)
        src, dst = (gathered.at[a, g, (y + dy) % 4, piece] for g in range(2))
        send(("x", a, dy, half), src, dst, (x_r, x_l)[half])

    def to_core(a, g, dy, half):
        piece = own_piece(a, g, dy, half)
        send(("s", a, g, dy, half), piece, piece, sib)

    def own_x(a):
        if a == 1:
            loads[a].wait()
        for half in range(2):
            across_x(a, 0, half)

    def own_y(a):
        if a == 0:
            loads[a].wait()
        for halves_of in ((0, 1), (1, 0)):
            for way in range(2):
                piece = own_piece(a, 0, 0, halves_of[way])
                send(("y", a, way, halves_of[way]), piece, piece, (y_r, y_l)[way])

    def gy(a, way, half):
        dy = 3 if way == 0 else 1
        piece = own_piece(a, 0, dy, half)
        arrive(("y", a, way, half), piece)
        if half == way:
            send(("yf", a, way), piece, piece, (y_r, y_l)[way])
        across_x(a, dy, half)
        to_core(a, 0, dy, half)

    def gf(a, way):
        arrive(("yf", a, way), own_piece(a, 0, 2, way))
        across_x(a, 2, way)
        to_core(a, 0, 2, way)

    def gx(a, dy, half):
        arrive(("x", a, dy, half), own_piece(a, 1, dy, half))
        to_core(a, 1, dy, half)

    def split_weights(a):
        loads[2 + a].wait()
        high, low = halves(raw[a])
        weights[a, 0:UNITS] = high
        weights[a, UNITS:2 * UNITS] = high
        weights[a, 2 * UNITS:3 * UNITS] = low

    def prod(u):
        def nt(left, right):
            return lax.dot_general(left, right, (((1,), (1,)), ((), ())), preferred_element_type=F32)

        def product(a, blocks):
            high, low = halves(jnp.concatenate([gathered[a, g, (y + dy) % 4] for g, dy in blocks], axis=0))
            w_high, w_low = weights[a, 0:UNITS], weights[a, 2 * UNITS:3 * UNITS]
            return nt(high, w_high) + (nt(low, w_high) + nt(high, w_low))

        for a, g, dy in GROUPS[u]:
            if (g, dy) != (0, 0):
                for half in range(2):
                    arrive(("s", a, g, dy, half), gathered.at[a, g, (y + dy) % 4, rows(1 - q, half)])
        for a in range(2):
            blocks = [block for block in GROUPS[u] if block[0] == a]
            if blocks:
                total = product(a, [block[1:] for block in blocks])
                for n, block in enumerate(blocks):
                    partial[:, PLACE[block]] = total[n * BLOCK:(n + 1) * BLOCK].reshape(8, CHUNK, UNITS)
        rs_send(u, FIRST_WAY[u], 1)
        rs_send(u, 1 - FIRST_WAY[u], 2)

    def z_chunk(way, distance):
        return (z + z_sgn[way] * distance) % 8

    def rs_send(u, way, step):
        src, dst = partial.at[z_chunk(way, 5 - step), SPAN[u]], summed.at[way, step - 1, SPAN[u]]
        send(("rs", u, way, step), src, dst, z_dev[way])

    def rs_hop(u, way, step):
        arrive(("rs", u, way, step - 1), summed.at[way, step - 2, SPAN[u]])
        c = z_chunk(way, 5 - step)
        partial[c, SPAN[u]] = partial[c, SPAN[u]] + summed[way, step - 2, SPAN[u]]
        rs_send(u, way, step)

    def ag_send(u, way, k):
        piece = spread.at[z_chunk(1 - way, k - 1), SPAN[u]]
        send(("ag", u, way, k), piece, piece, z_dev[way])

    def ag_get(u, way, k):
        arrive(("ag", u, way, k), spread.at[z_chunk(1 - way, k), SPAN[u]])
        if k < 3 or (k == 3 and way == FIRST_WAY[u]):
            ag_send(u, way, k + 1)

    def finish(u):
        for way in range(2):
            arrive(("rs", u, way, 4), summed.at[way, 3, SPAN[u]])
        for a, g, dy in GROUPS[u]:
            at = PLACE[(a, g, dy)]
            total = partial[z, at] + summed[0, 3, at] + summed[1, 3, at]
            if a == 0:
                spread[z, at], slope[g, dy] = gelu_parts(total)
            else:
                spread[z, at] = total * slope[g, dy]
        for way in range(2):
            ag_send(u, way, 1)

    def spread_rows(a, chunks):
        return jnp.concatenate([spread[c, PLACE[(a, g, dy)]] for c in chunks for g, dy in BLOCKS], axis=0)

    def round_chunk(r, core):
        if r == 4:
            return (z + 4 * core) % 8
        return (z + r + (8 - 2 * r) * core) % 8

    def f_mm(a, r, *cores):
        high, low = halves(spread_rows(a, [round_chunk(r, core) for core in cores]))
        total = jnp.dot(jnp.concatenate([high, low, high], axis=1), weights[1 - a], preferred_element_type=F32)
        for i, core in enumerate(cores):
            for n, (g, dy) in enumerate(BLOCKS):
                at = i * BLOCK + n * CHUNK
                for side in range(2):
                    fold[r - 1, a, core, side, g, (y + dy) % 4] = total[at:at + CHUNK, side * UNITS:(side + 1) * UNITS]
        if 1 in cores:
            send(("fs", a, r), fold.at[r - 1, a, 1 - q], from_sib.at[r - 1, a], sib)

    def f_sib(a, r):
        i = r - 1
        arrive(("fs", a, r), from_sib.at[i, a])
        fold[i, a, q] = fold[i, a, q] + from_sib[i, a]
        if Y_FIRST[a][i]:
            send(("f1", a, r, 0), fold.at[i, a, q, 0, :, (y + 2) % 4], near.at[i, a, 0], y_r)
            send(("f1", a, r, 1), fold.at[i, a, q, 1, :, (y + 2) % 4], near.at[i, a, 1], y_l)
        else:
            send(("f1", a, r, 0), fold.at[i, a, q, 1 - xh, 0, 0:2], near.at[i, a, 0], x_r)
            send(("f1", a, r, 1), fold.at[i, a, q, 1 - xh, 0, 2:4], near.at[i, a, 1], x_l)

    def f_r1(a, r):
        i = r - 1
        for way, yy, xx in ((0, (y + 1) % 4, xh_r), (1, (y + 3) % 4, xh_l)):
            arrive(("f1", a, r, way), near.at[i, a, way])
            if Y_FIRST[a][i]:
                fold[i, a, q, way, :, yy] = fold[i, a, q, way, :, yy] + near[i, a, way]
                send(("f2", a, r, way), fold.at[i, a, q, :, :, yy], far_y.at[i, a, way], (y_r, y_l)[way])
            else:
                half = slice(2 * way, 2 * way + 2)
                fold[i, a, q, xx, 1, half] = fold[i, a, q, xx, 1, half] + near[i, a, way]
                send(("f2", a, r, way), fold.at[i, a, q, xx, 1], far_x.at[i, a, way], (x_r, x_l)[way])

    def f_r2(a, r):
        i = r - 1
        far = (far_x, far_y)[Y_FIRST[a][i]]
        for way in range(2):
            arrive(("f2", a, r, way), far.at[i, a, way])
        if Y_FIRST[a][i]:
            fold[i, a, q, :, :, y] = fold[i, a, q, :, :, y] + far[i, a, 0] + far[i, a, 1]
            send(("f3", a, r), fold.at[i, a, q, 1 - xh, 0, y], last.at[i, a], x_s)
        else:
            fold[i, a, q, xh, 0] = fold[i, a, q, xh, 0] + far[i, a, 0] + far[i, a, 1]
            send(("f3", a, r), fold.at[i, a, q, xh, 0, (y + 2) % 4], last.at[i, a], y_s)

    def f_r3(a, r):
        i = r - 1
        arrive(("f3", a, r), last.at[i, a])
        if Y_FIRST[a][i]:
            fold[i, a, q, xh_s, 1, y] = fold[i, a, q, xh_s, 1, y] + last[i, a]
            send(("f4", a, r, 0), fold.at[i, a, q, xh_r, 1, y], ends.at[i, a, 0], x_r)
            send(("f4", a, r, 1), fold.at[i, a, q, xh_l, 1, y], ends.at[i, a, 1], x_l)
        else:
            ys = (y + 1 + 2 * q) % 4
            fold[i, a, q, xh, 0, ys] = fold[i, a, q, xh, 0, ys] + last[i, a]
            send(("f4", a, r, 0), fold.at[i, a, q, xh, 0, (y + 1) % 4], ends.at[i, a, 0], y_r)
            send(("f4", a, r, 1), fold.at[i, a, q, xh, 0, (y + 3) % 4], ends.at[i, a, 1], y_l)

    def f_r4(a, r):
        i = r - 1
        arrive(("f4", a, r, 0), ends.at[i, a, 0])
        arrive(("f4", a, r, 1), ends.at[i, a, 1])
        result[a, i] = fold[i, a, q, xh, 0, y] + ends[i, a, 0] + ends[i, a, 1]

    def swap(a):
        first, second = result[a, :, :, 0:BLOCK], result[a, :, :, BLOCK:2 * BLOCK]
        lower = jnp.full(first.shape, q, jnp.int32) == 0
        give[a] = jnp.where(lower, second, first)
        send(("swap", a), give.at[a], take.at[a], sib)
        mine = jnp.where(lower, first, second)
        for r in range(1, 5):
            at = pl.ds(pl.multiple_of(round_chunk(r, q) * CHUNK, 8), CHUNK)
            widths[a, at, :] = mine[r - 1]

    def swapped(a):
        arrive(("swap", a), take.at[a])
        for r in range(1, 5):
            at = pl.ds(pl.multiple_of(round_chunk(r, 1 - q) * CHUNK, 8), CHUNK)
            widths[a, at, :] = take[a, r - 1]
        stores[a].start()

    rounds_done = [0, 0]

    def grad(a, r):
        chunks = (round_chunk(r, 0), round_chunk(r, 1))
        left = spread_rows(a, chunks).T
        right = jnp.concatenate([
            gathered[1 - a, g, (y + dy) % 4, pl.ds(pl.multiple_of(c * CHUNK, 8), CHUNK), :]
            for c in chunks for g, dy in BLOCKS
        ], axis=0)
        l_high, l_low = halves(left)
        r_high, r_low = halves(right)
        term = jnp.dot(
            jnp.concatenate([l_high, l_low, l_high], axis=1), jnp.concatenate([r_high, r_high, r_low], axis=0),
            preferred_element_type=F32)
        grads[a] = term if rounds_done[a] == 0 else grads[a] + term
        rounds_done[a] += 1
        if rounds_done[a] == 4:
            stores[2 + a].start()

    def drain(count):
        for copy in pending[:count]:
            copy.wait_send()
        del pending[:count]

    loads = [
        pltpu.make_async_copy(src, dst, local_sem.at[i])
        for i, (src, dst) in enumerate((
            (tokens, gathered.at[0, 0, y]), (cotangent, gathered.at[1, 0, y]),
            (up_weight, raw.at[0]), (down_weight, raw.at[1]),
        ))
    ]
    stores = [
        pltpu.make_async_copy(src, dst, local_sem.at[4 + i])
        for i, (src, dst) in enumerate((
            (widths.at[0], output), (widths.at[1], grad_tokens), (grads.at[0], grad_down), (grads.at[1], grad_up),
        ))
    ]
    for load in loads:
        load.start()
    barrier = pltpu.get_barrier_semaphore()
    partners = (sib, y_r, y_l, x_r, x_l, z_r, z_l)
    for device in partners:
        pl.semaphore_signal(barrier, inc=1, device_id=device, device_id_type=pl.DeviceIdType.MESH)
    pl.semaphore_wait(barrier, len(partners))

    steps = (
        own_x, own_y, gy, gf, gx, split_weights, prod, rs_hop, finish, ag_get,
        f_mm, f_sib, f_r1, f_r2, f_r3, f_r4, swap, swapped, grad, drain,
    )
    for step, *at in ORDER:
        steps[step](*at)
    drain(len(pending))
    for store in stores:
        store.wait()
    assert len(slots) <= SLOTS, len(slots)


def copy_kernel(*refs):
    sources, targets, held, sem = refs[:4], refs[4:8], refs[8:12], refs[12]
    loads, stores = [], []
    for src, dst, hold in zip(sources, targets, held):
        parts = 4 if src.shape[0] == UNITS else 1
        size = src.shape[0] // parts
        for part in range(parts):
            at, n = pl.ds(part * size, size), len(loads)
            loads.append(pltpu.make_async_copy(src.at[at], hold.at[at], sem.at[0, n]))
            stores.append(pltpu.make_async_copy(hold.at[at], dst.at[at], sem.at[1, n]))
    for load in loads:
        load.start()
    for load, store in zip(loads, stores):
        load.wait()
        store.start()
    for store in stores:
        store.wait()


def shards(tokens, up_weight, down_weight, cotangent):
    anywhere, piece = pl.BlockSpec(memory_space=pl.ANY), (CHUNK, UNITS)
    shapes = (
        jax.ShapeDtypeStruct((BLOCK, BLOCK), F32),
        jax.ShapeDtypeStruct((BLOCK, BLOCK), F32),
        jax.ShapeDtypeStruct((UNITS, WIDTH), F32),
        jax.ShapeDtypeStruct((UNITS, WIDTH), F32),
    )
    results = pl.pallas_call(
        kernel,
        out_shape=shapes,
        in_specs=[anywhere] * 4,
        out_specs=(anywhere,) * 4,
        scratch_shapes=[
            pltpu.VMEM((2, 2, 4, BLOCK, WIDTH), F32),
            pltpu.VMEM((2, UNITS, WIDTH), F32),
            pltpu.VMEM((2, 3 * UNITS, WIDTH), BF16),
            pltpu.VMEM((8, 16) + piece, F32),
            pltpu.VMEM((2, 4, 16) + piece, F32),
            pltpu.VMEM((8, 16) + piece, F32),
            pltpu.VMEM((2, 4) + piece, F32),
            pltpu.VMEM((4, 2, 2, 2, 2, 4) + piece, F32),
            pltpu.VMEM((4, 2, 2, 2, 4) + piece, F32),
            pltpu.VMEM((4, 2, 2, 2) + piece, F32),
            pltpu.VMEM((4, 2, 2, 4) + piece, F32),
            pltpu.VMEM((4, 2, 2, 2, 2) + piece, F32),
            pltpu.VMEM((4, 2) + piece, F32),
            pltpu.VMEM((4, 2, 2) + piece, F32),
            pltpu.VMEM((2, 4) + piece, F32),
            pltpu.VMEM((2, 4, CHUNK, BLOCK), F32),
            pltpu.VMEM((2, 4, CHUNK, BLOCK), F32),
            pltpu.VMEM((2, BLOCK, BLOCK), F32),
            pltpu.VMEM((2, UNITS, WIDTH), F32),
            pltpu.SemaphoreType.DMA((SLOTS,)),
            pltpu.SemaphoreType.DMA((SLOTS,)),
            pltpu.SemaphoreType.DMA((8,)),
        ],
        compiler_params=pltpu.CompilerParams(
            collective_id=0, has_side_effects=True, vmem_limit_bytes=62 * 1024 * 1024),
        cost_estimate=pl.CostEstimate(flops=16_300_000_000, bytes_accessed=6_000_000, transcendentals=73728),
    )(tokens, up_weight, down_weight, cotangent)
    return pl.pallas_call(
        copy_kernel,
        out_shape=shapes,
        in_specs=[anywhere] * 4,
        out_specs=(anywhere,) * 4,
        scratch_shapes=[pltpu.VMEM(shape.shape, F32) for shape in shapes] + [pltpu.SemaphoreType.DMA((2, 10))],
    )(*results)


def solution(mesh):
    return jax.shard_map(
        shards,
        mesh=mesh,
        in_specs=(
            P("row", "col"),
            P(("row", "depth"), "col"),
            P(("row", "depth"), "col"),
            P("row", "col"),
        ),
        out_specs=(
            P("row", ("col", "depth")),
            P("row", ("col", "depth")),
            P(("row", "depth"), "col"),
            P(("row", "depth"), "col"),
        ),
        check_vma=False,
    )
```

profile of v0, /device:TPU:1, one launch (start us, length us, event | category | flops | bytes accessed | tf_op | source)
XLA Modules:
  0.0 139.2 jit_solution(8830726794456613277)
XLA Ops:
  0.6 135.6 %shard_map.75 = (f32[192,192]{1,0:T(8,128)}, f32[192,192]{1,0:T(8,128)}, f32[384,768]{1,0:T(8,128)}, f32[384,768]{1,0:T(8,128)}) custom-call(f32[192,768]{1,0:T(8,128)} %tokens.1, f32[384,768]{1,0:T(8,128)} %up_weight.1, f32[384,768]{1,0:T(8,128)} %down_weight.1, f32[192,768]{1,0:T(8,128)} %cotangent.1), custom_call_target="tpu_custom_call" | custom-call | flops 16300000256 | bytes 6000000 | tf_op jit(solution)/shard_map/pallas_call | solution.py:405
  136.3 2.7 %shard_map.76 = (f32[192,192]{1,0:T(8,128)}, f32[192,192]{1,0:T(8,128)}, f32[384,768]{1,0:T(8,128)}, f32[384,768]{1,0:T(8,128)}) custom-call(f32[192,192]{1,0:T(8,128)} %get-tuple-element.8.refs_0_, f32[192,192]{1,0:T(8,128)} %get-tuple-element.9.refs_1_, f32[384,768]{1,0:T(8,128)} %get-tuple-element.10.refs_2_, f32[384,768]{1,0:T(8,128)} %get-tuple-element.11.refs_3_), custom_call_target="tpu_custom_call" | custom-call | tf_op jit(solution)/shard_map/pallas_call | solution.py:438
where the time goes:
time: 139 us
  Pallas kernels  138 us (99%)
    pallas_call x1, Pallas kernels, shards(): pl.pallas_call(kernel, out_shape=shapes, in_specs=[anywhere] * 4, out_spe...  136 us

commit v1 on v0

--- a/solution.py
+++ b/solution.py
@@ -36,34 +36,34 @@
     (GX, 1, 0, 1), (GX, 1, 0, 0), (OWN_Y, 1), (RS_HOP, 0, 0, 3), (RS_HOP, 0, 1, 4), (PROD, 2), (GF, 0, 0), (GF, 0, 1),
     (RS_HOP, 0, 0, 4), (PROD, 1), (GX, 0, 1, 0), (RS_HOP, 2, 0, 2), (RS_HOP, 2, 1, 3), (GY, 1, 0, 0), (GX, 0, 3, 0),
     (GX, 0, 1, 1), (GX, 0, 3, 1), (FINISH, 0), (GY, 1, 0, 1), (GX, 0, 2, 1), (GY, 1, 1, 0), (RS_HOP, 1, 1, 2),
-    (RS_HOP, 1, 0, 3), (GX, 0, 2, 0), (GY, 1, 1, 1), (DRAIN, 16), (RS_HOP, 2, 1, 4), (RS_HOP, 2, 0, 3), (PROD, 3),
-    (GF, 1, 0), (GX, 1, 3, 0), (AG_GET, 0, 1, 1), (RS_HOP, 1, 1, 3), (DRAIN, 16), (RS_HOP, 1, 0, 4), (GX, 1, 3, 1),
-    (PROD, 4), (DRAIN, 16), (GX, 1, 1, 0), (DRAIN, 16), (RS_HOP, 2, 0, 4), (RS_HOP, 3, 0, 3), (RS_HOP, 3, 1, 2),
-    (RS_HOP, 1, 1, 4), (RS_HOP, 4, 0, 2), (GX, 1, 2, 0), (GF, 1, 1), (RS_HOP, 4, 1, 3), (FINISH, 2), (GX, 1, 1, 1),
-    (RS_HOP, 3, 0, 4), (RS_HOP, 3, 1, 3), (RS_HOP, 4, 0, 3), (FINISH, 1), (AG_GET, 2, 0, 1), (RS_HOP, 4, 1, 4),
-    (AG_GET, 2, 1, 1), (RS_HOP, 3, 1, 4), (RS_HOP, 4, 0, 4), (AG_GET, 1, 0, 1), (PROD, 6), (AG_GET, 1, 1, 1),
-    (GX, 1, 2, 1), (AG_GET, 2, 0, 2), (FINISH, 4), (FINISH, 3), (PROD, 5), (RS_HOP, 6, 0, 2), (AG_GET, 0, 0, 1),
-    (AG_GET, 2, 0, 3), (PROD, 7), (AG_GET, 4, 0, 1), (AG_GET, 1, 1, 2), (AG_GET, 2, 1, 2), (AG_GET, 3, 1, 1),
-    (AG_GET, 4, 1, 1), (AG_GET, 3, 0, 1), (F_MM, 0, 1, 0, 1), (RS_HOP, 5, 1, 2), (RS_HOP, 5, 0, 3), (AG_GET, 1, 0, 2),
-    (RS_HOP, 6, 1, 3), (F_SIB, 0, 1), (GRAD, 0, 1), (AG_GET, 0, 0, 2), (RS_HOP, 6, 0, 3), (F_MM, 0, 4, 0),
-    (AG_GET, 3, 1, 2), (AG_GET, 4, 1, 2), (AG_GET, 1, 1, 3), (AG_GET, 4, 0, 2), (F_R1, 0, 1), (RS_HOP, 7, 1, 2),
-    (AG_GET, 3, 0, 2), (RS_HOP, 7, 0, 3), (AG_GET, 0, 1, 2), (F_MM, 0, 2, 0, 1), (RS_HOP, 5, 1, 3), (AG_GET, 1, 0, 3),
-    (RS_HOP, 6, 1, 4), (F_R2, 0, 1), (F_SIB, 0, 2), (AG_GET, 0, 0, 3), (GRAD, 0, 2), (AG_GET, 4, 0, 3), (DRAIN, 16),
-    (RS_HOP, 7, 1, 3), (AG_GET, 2, 1, 3), (RS_HOP, 5, 0, 4), (RS_HOP, 6, 0, 4), (F_R1, 0, 2), (RS_HOP, 5, 1, 4),
-    (AG_GET, 4, 1, 3), (AG_GET, 3, 0, 3), (AG_GET, 2, 0, 4), (F_R3, 0, 1), (AG_GET, 0, 1, 3), (AG_GET, 3, 1, 3),
-    (F_MM, 0, 3, 0, 1), (RS_HOP, 7, 0, 4), (GRAD, 0, 3), (RS_HOP, 7, 1, 4), (AG_GET, 4, 0, 4), (AG_GET, 0, 0, 4),
-    (F_SIB, 0, 3), (AG_GET, 1, 1, 4), (F_R2, 0, 2), (FINISH, 5), (FINISH, 6), (AG_GET, 3, 1, 4), (F_MM, 0, 4, 1),
-    (FINISH, 7), (F_R4, 0, 1), (F_MM, 1, 4, 0), (AG_GET, 5, 0, 1), (F_R1, 0, 3), (AG_GET, 5, 1, 1), (F_SIB, 0, 4),
-    (AG_GET, 6, 0, 1), (AG_GET, 6, 1, 1), (GRAD, 0, 4), (AG_GET, 7, 1, 1), (AG_GET, 7, 0, 1), (AG_GET, 5, 0, 2),
-    (AG_GET, 5, 1, 2), (F_MM, 1, 1, 0, 1), (AG_GET, 6, 1, 2), (F_R3, 0, 2), (F_R2, 0, 3), (AG_GET, 6, 0, 2),
-    (F_R1, 0, 4), (AG_GET, 7, 1, 2), (AG_GET, 7, 0, 2), (F_MM, 1, 2, 0, 1), (AG_GET, 5, 1, 3), (GRAD, 1, 1),
-    (AG_GET, 6, 0, 3), (AG_GET, 7, 1, 3), (AG_GET, 5, 0, 3), (F_R4, 0, 2), (F_SIB, 1, 1), (AG_GET, 6, 1, 3),
-    (F_R3, 0, 3), (F_SIB, 1, 2), (AG_GET, 7, 0, 3), (F_MM, 1, 3, 0, 1), (F_R2, 0, 4), (AG_GET, 5, 1, 4),
-    (AG_GET, 7, 1, 4), (AG_GET, 6, 0, 4), (F_MM, 1, 4, 1), (F_R1, 1, 1), (F_SIB, 1, 3), (F_R1, 1, 2), (F_SIB, 1, 4),
-    (GRAD, 1, 2), (F_R2, 1, 1), (F_R3, 0, 4), (F_R4, 0, 3), (DRAIN, 16), (F_R1, 1, 3), (F_R1, 1, 4), (DRAIN, 16),
-    (GRAD, 1, 3), (F_R3, 1, 1), (F_R2, 1, 2), (F_R4, 0, 4), (F_R2, 1, 3), (SWAP, 0), (F_R2, 1, 4), (F_R3, 1, 2),
-    (DRAIN, 16), (F_R3, 1, 3), (F_R4, 1, 1), (F_R3, 1, 4), (GRAD, 1, 4), (F_R4, 1, 2), (F_R4, 1, 3), (F_R4, 1, 4),
-    (SWAP, 1), (DRAIN, 16), (SWAPPED, 0), (SWAPPED, 1),
+    (RS_HOP, 1, 0, 3), (DRAIN, 16), (GX, 0, 2, 0), (GY, 1, 1, 1), (DRAIN, 16), (RS_HOP, 2, 1, 4), (RS_HOP, 2, 0, 3),
+    (PROD, 3), (GF, 1, 0), (GX, 1, 3, 0), (AG_GET, 0, 1, 1), (RS_HOP, 1, 1, 3), (DRAIN, 16), (RS_HOP, 1, 0, 4),
+    (GX, 1, 3, 1), (PROD, 4), (DRAIN, 16), (DRAIN, 16), (RS_HOP, 2, 0, 4), (RS_HOP, 3, 0, 3), (GX, 1, 1, 0),
+    (GX, 1, 2, 0), (RS_HOP, 3, 1, 2), (GF, 1, 1), (RS_HOP, 1, 1, 4), (RS_HOP, 4, 0, 2), (FINISH, 2),
+    (RS_HOP, 3, 0, 4), (RS_HOP, 4, 1, 3), (RS_HOP, 4, 0, 3), (RS_HOP, 3, 1, 3), (GX, 1, 1, 1), (FINISH, 1),
+    (RS_HOP, 4, 1, 4), (AG_GET, 2, 0, 1), (AG_GET, 2, 1, 1), (RS_HOP, 4, 0, 4), (RS_HOP, 3, 1, 4), (AG_GET, 1, 0, 1),
+    (AG_GET, 0, 1, 2), (PROD, 6), (AG_GET, 2, 0, 2), (GX, 1, 2, 1), (FINISH, 4), (FINISH, 3), (PROD, 7),
+    (AG_GET, 1, 1, 1), (PROD, 5), (RS_HOP, 6, 0, 2), (AG_GET, 4, 0, 1), (AG_GET, 3, 1, 1), (AG_GET, 4, 1, 1),
+    (AG_GET, 0, 0, 1), (AG_GET, 3, 0, 1), (F_MM, 0, 1, 0, 1), (RS_HOP, 5, 1, 2), (AG_GET, 1, 0, 2), (RS_HOP, 6, 0, 3),
+    (AG_GET, 1, 1, 2), (AG_GET, 4, 0, 2), (RS_HOP, 5, 0, 3), (RS_HOP, 6, 1, 3), (AG_GET, 2, 0, 3), (RS_HOP, 7, 1, 2),
+    (F_SIB, 0, 1), (GRAD, 0, 1), (AG_GET, 0, 0, 2), (F_MM, 0, 4, 0), (AG_GET, 4, 1, 2), (AG_GET, 2, 1, 2),
+    (AG_GET, 3, 1, 2), (AG_GET, 3, 0, 2), (F_MM, 0, 2, 0, 1), (AG_GET, 1, 1, 3), (F_R1, 0, 1), (AG_GET, 1, 0, 3),
+    (RS_HOP, 5, 1, 3), (RS_HOP, 5, 0, 4), (F_SIB, 0, 2), (RS_HOP, 7, 1, 3), (AG_GET, 4, 1, 3), (GRAD, 0, 2),
+    (RS_HOP, 6, 1, 4), (AG_GET, 0, 1, 3), (RS_HOP, 7, 0, 3), (AG_GET, 0, 0, 3), (AG_GET, 2, 1, 3), (RS_HOP, 6, 0, 4),
+    (AG_GET, 3, 0, 3), (F_R1, 0, 2), (RS_HOP, 5, 1, 4), (AG_GET, 4, 0, 3), (AG_GET, 3, 1, 3), (F_R2, 0, 1),
+    (F_MM, 0, 3, 0, 1), (RS_HOP, 7, 1, 4), (RS_HOP, 7, 0, 4), (GRAD, 0, 3), (AG_GET, 1, 1, 4), (AG_GET, 2, 0, 4),
+    (AG_GET, 0, 0, 4), (FINISH, 5), (F_SIB, 0, 3), (FINISH, 6), (AG_GET, 3, 1, 4), (F_R2, 0, 2), (AG_GET, 4, 0, 4),
+    (F_MM, 0, 4, 1), (F_R3, 0, 1), (FINISH, 7), (F_MM, 1, 4, 0), (AG_GET, 5, 0, 1), (AG_GET, 5, 1, 1), (F_R1, 0, 3),
+    (F_SIB, 0, 4), (AG_GET, 6, 0, 1), (AG_GET, 6, 1, 1), (AG_GET, 7, 1, 1), (AG_GET, 7, 0, 1), (GRAD, 0, 4),
+    (AG_GET, 5, 1, 2), (AG_GET, 5, 0, 2), (F_MM, 1, 1, 0, 1), (AG_GET, 6, 1, 2), (AG_GET, 6, 0, 2), (F_R2, 0, 3),
+    (F_R1, 0, 4), (AG_GET, 7, 1, 2), (F_R3, 0, 2), (AG_GET, 7, 0, 2), (F_MM, 1, 2, 0, 1), (AG_GET, 5, 1, 3),
+    (GRAD, 1, 1), (AG_GET, 6, 0, 3), (F_SIB, 1, 1), (F_R4, 0, 1), (F_R3, 0, 3), (AG_GET, 7, 1, 3), (AG_GET, 6, 1, 3),
+    (AG_GET, 5, 0, 3), (AG_GET, 7, 0, 3), (F_MM, 1, 3, 0, 1), (F_R2, 0, 4), (F_SIB, 1, 2), (AG_GET, 5, 1, 4),
+    (AG_GET, 6, 0, 4), (AG_GET, 7, 1, 4), (F_MM, 1, 4, 1), (F_R1, 1, 1), (F_SIB, 1, 3), (DRAIN, 16), (F_R1, 1, 2),
+    (F_SIB, 1, 4), (GRAD, 1, 2), (F_R3, 0, 4), (F_R2, 1, 1), (F_R1, 1, 3), (F_R4, 0, 3), (F_R4, 0, 2), (F_R1, 1, 4),
+    (GRAD, 1, 3), (F_R3, 1, 1), (F_R2, 1, 2), (F_R4, 0, 4), (DRAIN, 16), (DRAIN, 16), (SWAP, 0), (F_R2, 1, 3),
+    (F_R2, 1, 4), (F_R3, 1, 2), (F_R4, 1, 1), (F_R3, 1, 3), (F_R3, 1, 4), (GRAD, 1, 4), (F_R4, 1, 2), (F_R4, 1, 3),
+    (F_R4, 1, 4), (SWAP, 1), (DRAIN, 16), (SWAPPED, 0), (SWAPPED, 1),
 )
 
 
@@ -123,28 +123,26 @@
     def own_piece(a, g, dy, half):
         return gathered.at[a, g, (y + dy) % 4, rows(q, half)]
 
+    def own_rows(a, half):
+        return (tokens, cotangent)[a].at[rows(q, half)]
+
     def across_x(a, dy, half):
-        piece = rows(q, half)
-        src, dst = (gathered.at[a, g, (y + dy) % 4, piece] for g in range(2))
-        send(("x", a, dy, half), src, dst, (x_r, x_l)[half])
+        src = own_rows(a, half) if dy == 0 else own_piece(a, 0, dy, half)
+        send(("x", a, dy, half), src, own_piece(a, 1, dy, half), (x_r, x_l)[half])
 
     def to_core(a, g, dy, half):
         piece = own_piece(a, g, dy, half)
         send(("s", a, g, dy, half), piece, piece, sib)
 
     def own_x(a):
-        if a == 1:
-            loads[a].wait()
         for half in range(2):
             across_x(a, 0, half)
 
     def own_y(a):
-        if a == 0:
-            loads[a].wait()
         for halves_of in ((0, 1), (1, 0)):
             for way in range(2):
-                piece = own_piece(a, 0, 0, halves_of[way])
-                send(("y", a, way, halves_of[way]), piece, piece, (y_r, y_l)[way])
+                half = halves_of[way]
+                send(("y", a, way, half), own_rows(a, half), own_piece(a, 0, 0, half), (y_r, y_l)[way])
 
     def gy(a, way, half):
         dy = 3 if way == 0 else 1
@@ -181,7 +179,9 @@
             return nt(high, w_high) + (nt(low, w_high) + nt(high, w_low))
 
         for a, g, dy in GROUPS[u]:
-            if (g, dy) != (0, 0):
+            if (g, dy) == (0, 0):
+                loads[a].wait()
+            else:
                 for half in range(2):
                     arrive(("s", a, g, dy, half), gathered.at[a, g, (y + dy) % 4, rows(1 - q, half)])
         for a in range(2):

time: 139 us -> 141 us (1.014)
  Pallas kernels: 138 us -> 140 us
    pallas_call x1, Pallas kernels: 136 us -> 138 us  [shards(): pl.pallas_call(kernel, out_shape=shapes, in_specs=[anywhere] * 4, out_spe...]
where the time goes in v1:
time: 141 us
  Pallas kernels  140 us (99%)
    pallas_call x1, Pallas kernels, shards(): pl.pallas_call(kernel, out_shape=shapes, in_specs=[anywhere] * 4, out_spe...  138 us

profile of v1, /device:TPU:1, one launch (start us, length us, event | category | flops | bytes accessed | tf_op | source)
XLA Modules:
  0.0 141.2 jit_solution(17868557165563301981)
XLA Ops:
  0.6 137.7 %shard_map.75 = (f32[192,192]{1,0:T(8,128)}, f32[192,192]{1,0:T(8,128)}, f32[384,768]{1,0:T(8,128)}, f32[384,768]{1,0:T(8,128)}) custom-call(f32[192,768]{1,0:T(8,128)} %tokens.1, f32[384,768]{1,0:T(8,128)} %up_weight.1, f32[384,768]{1,0:T(8,128)} %down_weight.1, f32[192,768]{1,0:T(8,128)} %cotangent.1), custom_call_target="tpu_custom_call" | custom-call | flops 16300000256 | bytes 6000000 | tf_op jit(solution)/shard_map/pallas_call | solution.py:405
  138.4 2.7 %shard_map.76 = (f32[192,192]{1,0:T(8,128)}, f32[192,192]{1,0:T(8,128)}, f32[384,768]{1,0:T(8,128)}, f32[384,768]{1,0:T(8,128)}) custom-call(f32[192,192]{1,0:T(8,128)} %get-tuple-element.8.refs_0_, f32[192,192]{1,0:T(8,128)} %get-tuple-element.9.refs_1_, f32[384,768]{1,0:T(8,128)} %get-tuple-element.10.refs_2_, f32[384,768]{1,0:T(8,128)} %get-tuple-element.11.refs_3_), custom_call_target="tpu_custom_call" | custom-call | tf_op jit(solution)/shard_map/pallas_call | solution.py:438

commit v2 on v0

--- a/solution.py
+++ b/solution.py
@@ -123,28 +123,26 @@
     def own_piece(a, g, dy, half):
         return gathered.at[a, g, (y + dy) % 4, rows(q, half)]
 
+    def own_rows(a, half):
+        return (tokens, cotangent)[a].at[rows(q, half)]
+
     def across_x(a, dy, half):
-        piece = rows(q, half)
-        src, dst = (gathered.at[a, g, (y + dy) % 4, piece] for g in range(2))
-        send(("x", a, dy, half), src, dst, (x_r, x_l)[half])
+        src = own_rows(a, half) if dy == 0 else own_piece(a, 0, dy, half)
+        send(("x", a, dy, half), src, own_piece(a, 1, dy, half), (x_r, x_l)[half])
 
     def to_core(a, g, dy, half):
         piece = own_piece(a, g, dy, half)
         send(("s", a, g, dy, half), piece, piece, sib)
 
     def own_x(a):
-        if a == 1:
-            loads[a].wait()
         for half in range(2):
             across_x(a, 0, half)
 
     def own_y(a):
-        if a == 0:
-            loads[a].wait()
         for halves_of in ((0, 1), (1, 0)):
             for way in range(2):
-                piece = own_piece(a, 0, 0, halves_of[way])
-                send(("y", a, way, halves_of[way]), piece, piece, (y_r, y_l)[way])
+                half = halves_of[way]
+                send(("y", a, way, half), own_rows(a, half), own_piece(a, 0, 0, half), (y_r, y_l)[way])
 
     def gy(a, way, half):
         dy = 3 if way == 0 else 1
@@ -181,7 +179,9 @@
             return nt(high, w_high) + (nt(low, w_high) + nt(high, w_low))
 
         for a, g, dy in GROUPS[u]:
-            if (g, dy) != (0, 0):
+            if (g, dy) == (0, 0):
+                loads[a].wait()
+            else:
                 for half in range(2):
                     arrive(("s", a, g, dy, half), gathered.at[a, g, (y + dy) % 4, rows(1 - q, half)])
         for a in range(2):

time: 139 us -> 139 us (level)
  no operation moved by 1% of the time
where the time goes in v2:
time: 139 us
  Pallas kernels  139 us (100%)
    pallas_call x1, Pallas kernels, shards(): pl.pallas_call(kernel, out_shape=shapes, in_specs=[anywhere] * 4, out_spe...  136 us

profile of v2, /device:TPU:1, one launch (start us, length us, event | category | flops | bytes accessed | tf_op | source)
XLA Modules:
  0.0 139.4 jit_solution(5301306318700284936)
XLA Ops:
  0.6 135.8 %shard_map.75 = (f32[192,192]{1,0:T(8,128)}, f32[192,192]{1,0:T(8,128)}, f32[384,768]{1,0:T(8,128)}, f32[384,768]{1,0:T(8,128)}) custom-call(f32[192,768]{1,0:T(8,128)} %tokens.1, f32[384,768]{1,0:T(8,128)} %up_weight.1, f32[384,768]{1,0:T(8,128)} %down_weight.1, f32[192,768]{1,0:T(8,128)} %cotangent.1), custom_call_target="tpu_custom_call" | custom-call | flops 16300000256 | bytes 6000000 | tf_op jit(solution)/shard_map/pallas_call | solution.py:405
  136.5 2.7 %shard_map.76 = (f32[192,192]{1,0:T(8,128)}, f32[192,192]{1,0:T(8,128)}, f32[384,768]{1,0:T(8,128)}, f32[384,768]{1,0:T(8,128)}) custom-call(f32[192,192]{1,0:T(8,128)} %get-tuple-element.8.refs_0_, f32[192,192]{1,0:T(8,128)} %get-tuple-element.9.refs_1_, f32[384,768]{1,0:T(8,128)} %get-tuple-element.10.refs_2_, f32[384,768]{1,0:T(8,128)} %get-tuple-element.11.refs_3_), custom_call_target="tpu_custom_call" | custom-call | tf_op jit(solution)/shard_map/pallas_call | solution.py:438
